TPU v7x, 256 devices: a whole 4x4x8 slice. The times are simulated.
256 devices in a mesh: stn: 128 (over z, x_lo, y, core), tm: 2 (over x_hi).
Axes of the slice: x: 4 (x_hi: 2, x_lo: 2; x = x_hi * 2 + x_lo), y: 4, z: 8, core: 2. Of those that a mesh axis runs over, the one named last changes fastest.
Arguments:
- samples: bfloat16 [512, 2, 2, 131072], P('stn', None, None, 'tm'), may hold values from -6 to 6
- taps: float32 [12, 4096], replicated, may hold values from -1.8 to 1.8
- codes: int32 [64, 512], replicated, may hold values from 0 to 4095
- flags: int32 [512], replicated, may hold values 0 or 1
Outputs:
- beams: bfloat16 [4096, 2, 32, 128], P('stn', None, 'tm')
All inputs are finite; a program needn't handle non-finite values.
Results may differ from a plain program's by a relative error of at most 0.0077.
Values may be sent and summed in bfloat16 or wider, within the bound.
No kernel may reach another device: no remote copies, remote signals or barrier semaphores. Data moves between devices by JAX's collectives and lax.ppermute only.
A program may use at most 64 MiB of HBM per device.

v0:
```python
import jax
import jax.numpy as jnp
from jax import lax
from jax.sharding import PartitionSpec as P

RADIX_A = 32
RADIX_B = 128


def from_behind(shard, axis, by):
    size = lax.axis_size(axis)
    pairs = [(i, i + by) for i in range(size) if 0 <= i + by < size]
    return lax.ppermute(shard, axis, pairs)


def dft_table(radix):
    indices = jnp.arange(radix, dtype=jnp.int32)
    angles = (indices[:, None] * indices[None, :] % radix).astype(jnp.float32) * (
        2.0 * jnp.pi / radix
    )
    cosine = jnp.cos(angles).astype(jnp.bfloat16)
    sine = jnp.sin(angles).astype(jnp.bfloat16)
    return jnp.stack(
        [jnp.stack([cosine, -sine], axis=1), jnp.stack([sine, cosine], axis=1)], axis=0
    )


def twiddle_table(outer, inner):
    length = outer * inner
    rows = jnp.arange(outer, dtype=jnp.int32)
    cols = jnp.arange(inner, dtype=jnp.int32)
    angles = (rows[:, None] * cols[None, :] % length).astype(jnp.float32) * (2.0 * jnp.pi / length)
    return (jnp.cos(angles), jnp.sin(angles))


def beam_weights(codes, flags, channels, length, stations_all):
    phase = channels[:, :, None, None] * jnp.transpose(codes)[None, None, :, :] % length
    angles = phase.astype(jnp.float32) * (2.0 * jnp.pi / length)
    scale = flags.astype(jnp.float32) / jnp.sqrt(jnp.float32(stations_all))
    real_part = (jnp.cos(angles) * scale[None, None, :, None]).astype(jnp.bfloat16)
    imag_part = (-jnp.sin(angles) * scale[None, None, :, None]).astype(jnp.bfloat16)
    first_row = jnp.stack([real_part, imag_part], axis=3)
    second_row = jnp.stack([-imag_part, real_part], axis=3)
    return jnp.stack([first_row, second_row], axis=2)


def shards(samples, taps, codes, flags):
    stn_local = samples.shape[0]
    tap_count = taps.shape[0]
    length = taps.shape[1]
    outer = RADIX_A
    inner = RADIX_B
    frame_count = samples.shape[3] // length
    frames = samples.reshape(stn_local, 2, 2, frame_count, outer, inner)
    history = from_behind(frames[:, :, :, frame_count - (tap_count - 1) :], "tm", 1)
    padded = jnp.concatenate([history, frames], axis=3)
    taps_grid = taps.reshape(tap_count, outer, inner)
    filtered = jnp.zeros((stn_local, 2, 2, frame_count, outer, inner), jnp.float32)
    for tap in range(tap_count):
        filtered = filtered + taps_grid[tap][None, None, None, None] * padded[
            :, :, :, tap : tap + frame_count
        ].astype(jnp.float32)
    filtered = filtered.astype(jnp.bfloat16)
    table_outer = dft_table(outer)
    table_inner = dft_table(inner).reshape(2 * inner, 2 * inner)
    tw_cos, tw_sin = twiddle_table(outer, inner)
    tw_cos = tw_cos[:, None, None, None, :]
    tw_sin = tw_sin[:, None, None, None, :]
    norm = jnp.sqrt(jnp.float32(length))
    first = jnp.einsum(
        "iaoc,spifab->ocspfb", table_outer, filtered, preferred_element_type=jnp.float32
    )
    real_in = first[0]
    imag_in = first[1]
    real_out = (real_in * tw_cos + imag_in * tw_sin) / norm
    imag_out = (imag_in * tw_cos - real_in * tw_sin) / norm
    middle = jnp.concatenate([real_out, imag_out], axis=-1).astype(jnp.bfloat16)
    second = jnp.einsum("cspfk,kn->cspfn", middle, table_inner, preferred_element_type=jnp.float32)
    spectra = second.astype(jnp.bfloat16).reshape(outer, stn_local, 2, frame_count, 2, inner)
    digits = inner // lax.axis_size("stn")
    upper = lax.axis_index("stn") * digits + jnp.arange(digits, dtype=jnp.int32)
    channels = jnp.arange(outer, dtype=jnp.int32)[None, :] + outer * upper[:, None]
    stations_all = codes.shape[1]
    beam_count = codes.shape[0]
    weights = beam_weights(codes, flags, channels, length, stations_all)
    turned = lax.all_to_all(spectra, "stn", split_axis=5, concat_axis=1, tiled=True)
    result = jnp.einsum(
        "cspfoe,ecosrb->ecpfrb", turned, weights, preferred_element_type=jnp.float32
    )
    return result.reshape(digits * outer, 2, turned.shape[3], 2 * beam_count).astype(jnp.bfloat16)


def solution(mesh):
    in_specs = (P("stn", None, None, "tm"), P(), P(), P())
    out_specs = P("stn", None, "tm", None)
    return jax.shard_map(shards, mesh=mesh, in_specs=in_specs, out_specs=out_specs, check_vma=False)
```

profile of v0, /device:TPU:7, one launch (start us, length us, event | category | flops | bytes accessed | tf_op | source)
XLA Modules:
  0.0 171.2 jit_solution(11299359552949289476)
XLA Ops:
  0.0 4.9 %reshape.358 = bf16[4,2,2,16,32,128]{5,4,3,2,1,0:T(8,128)(2,1)S(1)} reshape(bf16[4,2,2,65536]{3,2,1,0:T(2,128)(2,1)} %param.4) | data formatting | bytes 4194304 | tf_op jit(solution)/shard_map/reshape | solution.py:54
  4.9 0.3 slice.116
  5.2 0.4 copy.57
  5.6 1.3 collective-permute-start
  6.9 0.3 sine_convert_fusion
  7.2 0.3 fusion.35
  7.5 0.8 copy.34
  8.3 1.6 reshape.366
  10.0 0.1 fusion.38
  10.0 0.1 sine_convert_fusion.1
  10.1 0.1 fusion.36
  10.2 2.0 %fusion.43 = (f32[1,4096]{1,0:T(1,128)S(1)}, f32[1,4096]{1,0:T(1,128)S(1)}, f32[1,4096]{1,0:T(1,128)S(1)}, f32[1,4096]{1,0:T(1,128)S(1)}, f32[1,4096]{1,0:T(1,12...) fusion(f32[12,4096]{1,0:T(8,128)} %param.5), kind=kLoop, calls=%fused_computation.81 | loop fusion | bytes 393216 | tf_op jit(solution)/shard_map/slice | solution.py:60
  12.2 29.3 %collective-permute-done = bf16[4,2,2,11,32,128]{5,4,2,3,1,0:T(8,128)(2,1)} collective-permute-done((bf16[4,2,2,11,32,128]{5,4,2,3,1,0:T(8,128)(2,1)S(1)}, bf16[4,2,2,11,32,128]{5,4,2,3,1,0:T(8,128)(2,1)}, u32[]{:S(2)}, u32[]{:S(2)}) %collective-permute-start) | collective-permute-done | bytes 1441824 | tf_op jit(solution)/shard_map/ppermute | solution.py:13
  41.6 1.8 %constant_dynamic-update-slice_fusion.1 = bf16[4,2,2,27,32,128]{5,4,2,3,1,0:T(8,128)(2,1)S(1)} fusion(bf16[4,2,2,11,32,128]{5,4,2,3,1,0:T(8,128)(2,1)} %collective-permute-done), kind=kLoop, calls=%fused_computation.73 | loop fusion | bytes 2883584
  43.4 0.8 constant_dynamic-update-slice_fusion
  44.2 4.6 %convolution_bitcast_fusion = f32[2,32,4,2,16,128]{5,1,4,3,2,0:T(8,128)S(1)} fusion(bf16[4,2,2,27,32,128]{5,4,2,3,1,0:T(8,128)(2,1)S(1)} %constant_dynamic-update-slice_fusion, f32[32,128]{1,0:T(8,128)S(1)} %bitcast.96, f32[32,128]{1,0:T(8,128)S(1)} %bitcast.97, f32[32,128]{1,0:T(8,128)S(1)} %bitcast.87, f32[32,128]{1,0:T(8,128)S(1)} %bitcast.88, ...), kind=kOutput, calls=%fused_computation.17 | convolution fusion | flops 171982848 | bytes 29589504 | tf_op jit(solution)/shard_map/iaoc,spifab->ocspfb/dot_general | solution.py:70
  48.8 0.0 copy-start.1
  48.8 0.7 multiply_convert_fusion.3
  49.5 0.3 pad_maximum_fusion
  49.8 0.0 copy-done.1
  49.8 3.8 %fusion.9 = bf16[32,4,2,16,256]{4,3,2,1,0:T(8,128)(2,1)} fusion(bf16[32,4,2,16,256]{4,0,3,2,1:T(8,128)(2,1)S(1)} %pad_maximum_fusion, bf16[256,256,1,1,1]{1,0,2,3,4:T(8,128)(2,1)S(1)} %copy-done.1), kind=kOutput, calls=%fused_computation.26 | convolution fusion | flops 537919488 | bytes 4325376 | tf_op jit(solution)/shard_map/cspfk,kn->cspfn/dot_general | solution.py:78
  53.6 2.5 %reshape.360 = bf16[32,4,2,16,2,128]{5,4,3,2,1,0:T(2,128)(2,1)S(1)} reshape(bf16[32,4,2,16,256]{4,3,2,1,0:T(8,128)(2,1)} %fusion.9) | data formatting | bytes 4194304 | tf_op jit(solution)/shard_map/reshape | solution.py:79
  56.2 11.0 %copy.36 = bf16[32,4,2,16,2,128]{0,3,4,2,1,5:T(8,128)(2,1)} copy(bf16[32,4,2,16,2,128]{5,4,3,2,1,0:T(2,128)(2,1)S(1)} %reshape.360) | data formatting | bytes 4194304 | tf_op jit(solution)/shard_map/reshape | solution.py:79
  67.2 12.8 %reshape.371 = bf16[128,2,4096]{2,1,0:T(2,128)(2,1)} reshape(bf16[128,4,2,2,16,32]{5,4,3,2,1,0:T(8,128)(2,1)} %bitcast.82) | data formatting | bytes 4194304
  80.0 0.0 copy-start.2
  80.0 0.0 copy-start
  80.0 15.2 %all-to-all-start = ((bf16[128,2,4096]{2,1,0:T(2,128)(2,1)}), bf16[128,2,4096]{2,1,0:T(2,128)(2,1)S(1)}, u32[]{:S(2)}, u32[]{:S(2)}) async-start(bf16[128,2,4096]{2,1,0:T(2,128)(2,1)} %reshape.371), calls=%async_computation | async-start | bytes 4194304 | tf_op jit(solution)/shard_map/all_to_all | solution.py:86
  95.3 0.0 copy-done.2
  95.3 0.0 copy-done
  95.3 16.5 %fusion.41 = bf16[1,32,512,1,64]{2,4,3,1,0:T(8,128)(2,1)S(1)} fusion(f32[512]{0:T(512)S(1)} %convert_multiply_fusion, s32[512,64]{0,1:T(8,128)S(1)} %bitcast.84, s32[32]{0:T(128)S(1)} %iota_add_fusion), kind=kLoop, calls=%fused_computation.79 | loop fusion | flops 20971520 | bytes 2230400 | tf_op jit(solution)/shard_map/neg | solution.py:43
  111.8 17.7 %multiply_convert_fusion = (bf16[1,32,512,1,64]{2,4,3,1,0:T(8,128)(2,1)S(1)}, bf16[1,32,512,1,64]{2,4,3,1,0:T(8,128)(2,1)S(1)}) fusion(f32[512]{0:T(512)S(1)} %convert_multiply_fusion, s32[512,64]{0,1:T(8,128)S(1)} %bitcast.85, s32[32]{0:T(128)S(1)} %iota_add_fusion), kind=kLoop, calls=%fused_computation.14 | loop fusion | flops 19922944 | bytes 4327552 | tf_op jit(solution)/shard_map/convert_element_type | solution.py:41
  129.6 3.5 %maximum_bitcast_fusion.2 = (bf16[1,32,1,512,2,64]{3,5,2,4,1,0:T(8,128)(2,1)}, bf16[1,32,1,512,2,64]{3,5,2,4,1,0:T(8,128)(2,1)}) fusion(bf16[1,32,512,1,64]{2,4,3,1,0:T(8,128)(2,1)S(1)} %get-tuple-element.21, bf16[1,32,512,1,64]{2,4,3,1,0:T(8,128)(2,1)S(1)} %get-tuple-element.22, bf16[1,32,512,1,64]{2,4,3,1,0:T(8,128)(2,1)S(1)} %fusion.41), kind=kLoop, calls=%fused_computation.12 | loop fusion | flops 4194304 | bytes 14680064 | tf_op jit(solution)/shard_map/stack | solution.py:44
  133.1 14.0 %all-to-all-done = bf16[128,2,4096]{2,1,0:T(2,128)(2,1)S(1)} async-done(((bf16[128,2,4096]{2,1,0:T(2,128)(2,1)}), bf16[128,2,4096]{2,1,0:T(2,128)(2,1)S(1)}, u32[]{:S(2)}, u32[]{:S(2)}) %all-to-all-start) | async-done | bytes 2097184 | tf_op jit(solution)/shard_map/all_to_all | solution.py:86
  147.1 6.6 %reshape.372 = bf16[128,4,2,2,16,32]{5,4,3,2,1,0:T(8,128)(2,1)} reshape(bf16[128,2,4096]{2,1,0:T(2,128)(2,1)S(1)} %all-to-all-done) | data formatting | bytes 4194304
  153.7 9.6 %copy.43 = bf16[32,512,2,16,2,1]{1,3,4,5,2,0:T(8,128)(2,1)S(1)} copy(bf16[32,512,2,16,2,1]{0,3,4,2,1,5:T(8,128)(2,1)} %bitcast.83) | data formatting | bytes 4194304 | tf_op jit(solution)/shard_map/reshape.34
  163.3 6.4 %fusion.13 = bf16[32,2,16,2,64]{4,2,3,1,0:T(8,128)(2,1)S(1)} fusion(bf16[32,512,2,16,2,1]{1,3,4,5,2,0:T(8,128)(2,1)S(1)} %copy.43, bf16[1,32,1,512,2,64]{3,5,2,4,1,0:T(8,128)(2,1)} %get-tuple-element.8, bf16[1,32,1,512,2,64]{3,5,2,4,1,0:T(8,128)(2,1)} %get-tuple-element.7), kind=kOutput, calls=%fused_computation.28 | convolution fusion | flops 285343744 | bytes 10747904 | tf_op jit(solution)/shard_map/cspfoe,ecosrb->ecpfrb/dot_general | solution.py:87
  169.7 0.5 copy.39
  170.3 1.0 convert_element_type.249
  (5 shorter events, 0.0 us)
Async XLA Ops:
  5.6 36.0 %collective-permute-start = (bf16[4,2,2,11,32,128]{5,4,2,3,1,0:T(8,128)(2,1)S(1)}, bf16[4,2,2,11,32,128]{5,4,2,3,1,0:T(8,128)(2,1)}, u32[]{:S(2)}, u32[]{:S(2)}) collective-permute-start(bf16[4,2,2,11,32,128]{5,4,2,3,1,0:T(8,128)(2,1)S(1)} %copy.57), channel_id=1, source_target_pairs={{0,1},{2,3},{4,5},{6,7},{8,9},{10,11},{12,13},{14,15},{16,17},{18,... | collective-permute-start | bytes 4325384 | tf_op jit(solution)/shard_map/ppermute | solution.py:13
  48.8 1.1 copy-start.1
  80.0 15.2 %copy-start.2 = (s32[512]{0:T(512)S(1)}, s32[512]{0:T(512)}, u32[]{:S(2)}) copy-start(s32[512]{0:T(512)} %param.7) | copy-start | bytes 6148
  80.0 15.3 %copy-start = (s32[64,512]{1,0:T(8,128)S(1)}, s32[64,512]{1,0:T(8,128)}, u32[]{:S(2)}) copy-start(s32[64,512]{1,0:T(8,128)} %param.6) | copy-start | bytes 393220
  80.0 67.0 %all-to-all-start = ((bf16[128,2,4096]{2,1,0:T(2,128)(2,1)}), bf16[128,2,4096]{2,1,0:T(2,128)(2,1)S(1)}, u32[]{:S(2)}, u32[]{:S(2)}) async-start(bf16[128,2,4096]{2,1,0:T(2,128)(2,1)} %reshape.371), calls=%async_computation | async-start | bytes 4194304 | tf_op jit(solution)/shard_map/all_to_all | solution.py:86
where the time goes:
time: 172 us; the launch traced here: 171 us
  local copies, waits for them, and re-layouts  56.7 us (33%)
  waiting for transfers between devices  43.3 us (25%)
  other arithmetic  39.7 us (23%)
  starting transfers between devices  16.5 us (10%)
  matrix products  14.8 us (9%)
    ppermute x1, waiting for transfers between devices, from_behind(): return lax.ppermute(shard, axis, pairs)  29.3 us
    unnamed x10, local copies, waits for them, and re-layouts  21.6 us
    convert_element_type x1, other arithmetic, beam_weights(): (-jnp.sin(angles) * scale[None, None, :, None]).astype(jnp.bfloat16)  17.7 us
    neg x1, other arithmetic, beam_weights(): second_row = jnp.stack([-imag_part, real_part], axis=3)  16.5 us
    all_to_all x1, starting transfers between devices, shards(): lax.all_to_all(spectra, 'stn', split_axis=5, concat_axis=1, tiled=True)  15.2 us
    all_to_all x1, waiting for transfers between devices, shards(): lax.all_to_all(spectra, 'stn', split_axis=5, concat_axis=1, tiled=True)  14 us
    reshape x2, local copies, waits for them, and re-layouts, shards(): second.astype(jnp.bfloat16)  13.6 us
    another operation x1, local copies, waits for them, and re-layouts  9.62 us
  transfers between devices with their start and end apart: 2, of which 2 were waited for; matrix products, arithmetic and copies ran while one was open for 25% of the time, Pallas kernels for 0%

commit v1 on v0

--- a/solution.py
+++ b/solution.py
@@ -83,7 +83,10 @@
     stations_all = codes.shape[1]
     beam_count = codes.shape[0]
     weights = beam_weights(codes, flags, channels, length, stations_all)
-    turned = lax.all_to_all(spectra, "stn", split_axis=5, concat_axis=1, tiled=True)
+    turned = jnp.concatenate(
+        lax.all_to_all(jnp.stack(jnp.split(spectra, lax.axis_size("stn"), axis=5)), "stn", 0, 0),
+        axis=1,
+    )
     result = jnp.einsum(
         "cspfoe,ecosrb->ecpfrb", turned, weights, preferred_element_type=jnp.float32
     )

time: 172 us -> 303 us (1.76)
  local copies, waits for them, and re-layouts: 56.7 us -> 187 us
    unnamed x10 -> x139, local copies, waits for them, and re-layouts: 21.6 us -> 155 us
    reshape x2 -> x1, local copies, waits for them, and re-layouts: 13.6 us -> 9.33 us  [shards(): second.astype(jnp.bfloat16)]
    another operation x1 -> x2, local copies, waits for them, and re-layouts: 9.62 us -> 10.2 us
  transfers between devices with their start and end apart: 2 -> 2, of which waited for: 2 -> 2; matrix products, arithmetic and copies ran while one was open for 25% -> 14% of each run, Pallas kernels for 0% -> 0%
where the time goes in v1:
time: 303 us; the launch traced here: 300 us
  local copies, waits for them, and re-layouts  187 us (62%)
  waiting for transfers between devices  43.3 us (14%)
  other arithmetic  39.7 us (13%)
  starting transfers between devices  16.4 us (5%)
  matrix products  13.5 us (4%)
    unnamed x139, local copies, waits for them, and re-layouts  155 us
    ppermute x1, waiting for transfers between devices, from_behind(): return lax.ppermute(shard, axis, pairs)  29.4 us
    convert_element_type x1, other arithmetic, beam_weights(): (-jnp.sin(angles) * scale[None, None, :, None]).astype(jnp.bfloat16)  17.7 us
    neg x1, other arithmetic, beam_weights(): second_row = jnp.stack([-imag_part, real_part], axis=3)  16.5 us
    all_to_all x1, starting transfers between devices, shards(): lax.all_to_all(jnp.stack(jnp.split(spectra, lax.axis_size('stn'), axis=5)...  15.1 us
    all_to_all x1, waiting for transfers between devices, shards(): lax.all_to_all(jnp.stack(jnp.split(spectra, lax.axis_size('stn'), axis=5)...  14 us
    another operation x1, local copies, waits for them, and re-layouts  9.62 us
    reshape x1, local copies, waits for them, and re-layouts, shards(): second.astype(jnp.bfloat16)  9.33 us
  transfers between devices with their start and end apart: 2, of which 2 were waited for; matrix products, arithmetic and copies ran while one was open for 14% of the time, Pallas kernels for 0%

profile of v1, /device:TPU:7, one launch (start us, length us, event | category | flops | bytes accessed | tf_op | source)
XLA Modules:
  0.0 299.8 jit_solution(9372970287824154678)
XLA Ops:
  0.0 4.9 %reshape.362 = bf16[4,2,2,16,32,128]{5,4,3,2,1,0:T(8,128)(2,1)S(1)} reshape(bf16[4,2,2,65536]{3,2,1,0:T(2,128)(2,1)} %param.4) | data formatting | bytes 4194304 | tf_op jit(solution)/shard_map/reshape | solution.py:54
  8.3 1.6 reshape.371
  10.2 2.0 fusion.43
  12.2 29.4 %collective-permute-done = bf16[4,2,2,11,32,128]{5,4,2,3,1,0:T(8,128)(2,1)} collective-permute-done((bf16[4,2,2,11,32,128]{5,4,2,3,1,0:T(8,128)(2,1)S(1)}, bf16[4,2,2,11,32,128]{5,4,2,3,1,0:T(8,128)(2,1)}, u32[]{:S(2)}, u32[]{:S(2)}) %collective-permute-start) | collective-permute-done | bytes 1441824 | tf_op jit(solution)/shard_map/ppermute | solution.py:13
  41.6 1.8 constant_dynamic-update-slice_fusion.1
  44.2 4.6 %convolution_bitcast_fusion = f32[2,32,4,2,16,128]{5,1,4,3,2,0:T(8,128)S(1)} fusion(bf16[4,2,2,27,32,128]{5,4,2,3,1,0:T(8,128)(2,1)S(1)} %constant_dynamic-update-slice_fusion, f32[32,128]{1,0:T(8,128)S(1)} %bitcast.732, f32[32,128]{1,0:T(8,128)S(1)} %bitcast.733, f32[32,128]{1,0:T(8,128)S(1)} %bitcast.723, f32[32,128]{1,0:T(8,128)S(1)} %bitcast.724, ...), kind=kOutput, calls=%fused_computation.17 | convolution fusion | flops 171982848 | bytes 29589504 | tf_op jit(solution)/shard_map/iaoc,spifab->ocspfb/dot_general | solution.py:70
  49.8 2.4 fusion.9
  52.3 9.3 %copy.1626 = bf16[32,4,2,16,256]{0,3,4,2,1:T(8,128)(2,1)} copy(bf16[32,4,2,16,256]{4,3,2,1,0:T(8,128)(2,1)S(1)} %fusion.9) | data formatting | bytes 4194304 | tf_op jit(solution)/shard_map/reshape | solution.py:79
  61.6 1.6 constant_dynamic-update-slice_fusion.129
  63.2 1.9 constant_dynamic-update-slice_fusion.128
  65.1 1.5 constant_dynamic-update-slice_fusion.127
  68.0 1.5 constant_dynamic-update-slice_fusion.125
  69.5 1.5 constant_dynamic-update-slice_fusion.124
  71.0 1.5 constant_dynamic-update-slice_fusion.123
  72.4 1.5 constant_dynamic-update-slice_fusion.122
  73.9 1.5 constant_dynamic-update-slice_fusion.121
  75.4 1.5 constant_dynamic-update-slice_fusion.120
  76.8 1.5 constant_dynamic-update-slice_fusion.119
  78.3 1.5 constant_dynamic-update-slice_fusion.118
  79.7 1.5 constant_dynamic-update-slice_fusion.117
  81.2 1.5 constant_dynamic-update-slice_fusion.116
  85.6 1.5 constant_dynamic-update-slice_fusion.113
  90.0 1.5 constant_dynamic-update-slice_fusion.110
  91.4 1.5 constant_dynamic-update-slice_fusion.109
  94.4 1.5 constant_dynamic-update-slice_fusion.107
  97.3 1.5 constant_dynamic-update-slice_fusion.105
  98.8 1.5 constant_dynamic-update-slice_fusion.104
  100.2 1.5 constant_dynamic-update-slice_fusion.103
  101.7 1.5 constant_dynamic-update-slice_fusion.102
  103.1 1.5 constant_dynamic-update-slice_fusion.101
  104.6 1.5 constant_dynamic-update-slice_fusion.100
  106.1 1.5 constant_dynamic-update-slice_fusion.99
  109.0 1.5 constant_dynamic-update-slice_fusion.97
  110.5 1.5 constant_dynamic-update-slice_fusion.96
  111.9 1.5 constant_dynamic-update-slice_fusion.95
  113.4 1.5 constant_dynamic-update-slice_fusion.94
  116.3 1.5 constant_dynamic-update-slice_fusion.92
  117.8 1.5 constant_dynamic-update-slice_fusion.91
  122.2 1.5 constant_dynamic-update-slice_fusion.88
  123.6 1.5 constant_dynamic-update-slice_fusion.87
  126.6 1.5 constant_dynamic-update-slice_fusion.85
  128.0 1.5 constant_dynamic-update-slice_fusion.84
  130.9 1.5 constant_dynamic-update-slice_fusion.82
  133.9 1.5 constant_dynamic-update-slice_fusion.80
  135.3 1.5 constant_dynamic-update-slice_fusion.79
  138.2 1.5 constant_dynamic-update-slice_fusion.77
  139.7 1.5 constant_dynamic-update-slice_fusion.76
  141.2 1.5 constant_dynamic-update-slice_fusion.75
  142.6 1.5 constant_dynamic-update-slice_fusion.74
  144.1 1.5 constant_dynamic-update-slice_fusion.73
  147.0 1.5 constant_dynamic-update-slice_fusion.71
  148.5 1.5 constant_dynamic-update-slice_fusion.70
  150.0 1.5 constant_dynamic-update-slice_fusion.69
  151.4 1.5 constant_dynamic-update-slice_fusion.68
  154.4 1.5 constant_dynamic-update-slice_fusion.66
  196.0 12.8 %reshape.376 = bf16[128,2,4096]{2,1,0:T(2,128)(2,1)} reshape(bf16[128,4,2,2,1,16,32]{6,5,4,3,2,1,0:T(8,128)(2,1)} %bitcast.588) | data formatting | bytes 4194304
  208.8 15.1 %all-to-all-start = ((bf16[128,2,4096]{2,1,0:T(2,128)(2,1)}), bf16[128,2,4096]{2,1,0:T(2,128)(2,1)S(1)}, u32[]{:S(2)}, u32[]{:S(2)}) async-start(bf16[128,2,4096]{2,1,0:T(2,128)(2,1)} %reshape.376), calls=%async_computation | async-start | bytes 4194304 | tf_op jit(solution)/shard_map/all_to_all | solution.py:87
  223.9 16.5 %fusion.41 = bf16[1,32,512,1,64]{2,4,3,1,0:T(8,128)(2,1)S(1)} fusion(f32[512]{0:T(512)S(1)} %convert_multiply_fusion, s32[512,64]{0,1:T(8,128)S(1)} %bitcast.720, s32[32]{0:T(128)S(1)} %iota_add_fusion), kind=kLoop, calls=%fused_computation.335 | loop fusion | flops 20971520 | bytes 2230400 | tf_op jit(solution)/shard_map/neg | solution.py:43
  240.5 17.7 %multiply_convert_fusion = (bf16[1,32,512,1,64]{2,4,3,1,0:T(8,128)(2,1)S(1)}, bf16[1,32,512,1,64]{2,4,3,1,0:T(8,128)(2,1)S(1)}) fusion(f32[512]{0:T(512)S(1)} %convert_multiply_fusion, s32[512,64]{0,1:T(8,128)S(1)} %bitcast.721, s32[32]{0:T(128)S(1)} %iota_add_fusion), kind=kLoop, calls=%fused_computation.14 | loop fusion | flops 19922944 | bytes 4327552 | tf_op jit(solution)/shard_map/convert_element_type | solution.py:41
  258.2 3.5 %maximum_bitcast_fusion.2 = (bf16[1,32,1,512,2,64]{3,5,2,4,1,0:T(8,128)(2,1)}, bf16[1,32,1,512,2,64]{3,5,2,4,1,0:T(8,128)(2,1)}) fusion(bf16[1,32,512,1,64]{2,4,3,1,0:T(8,128)(2,1)S(1)} %get-tuple-element.21, bf16[1,32,512,1,64]{2,4,3,1,0:T(8,128)(2,1)S(1)} %get-tuple-element.22, bf16[1,32,512,1,64]{2,4,3,1,0:T(8,128)(2,1)S(1)} %fusion.41), kind=kLoop, calls=%fused_computation.12 | loop fusion | flops 4194304 | bytes 14680064 | tf_op jit(solution)/shard_map/stack | solution.py:44
  261.7 14.0 %all-to-all-done = bf16[128,2,4096]{2,1,0:T(2,128)(2,1)S(1)} async-done(((bf16[128,2,4096]{2,1,0:T(2,128)(2,1)}), bf16[128,2,4096]{2,1,0:T(2,128)(2,1)S(1)}, u32[]{:S(2)}, u32[]{:S(2)}) %all-to-all-start) | async-done | bytes 2097184 | tf_op jit(solution)/shard_map/all_to_all | solution.py:87
  275.7 6.5 %reshape.377 = bf16[128,4,2,2,1,16,32]{6,5,4,3,2,1,0:T(8,128)(2,1)} reshape(bf16[128,2,4096]{2,1,0:T(2,128)(2,1)S(1)} %all-to-all-done) | data formatting | bytes 4194304
  282.2 9.6 %copy.1621 = bf16[32,512,2,16,2,1]{1,3,4,5,2,0:T(8,128)(2,1)S(1)} copy(bf16[32,512,2,16,2,1]{0,3,4,2,1,5:T(8,128)(2,1)} %bitcast.719) | data formatting | bytes 4194304 | tf_op jit(solution)/shard_map/reshape.36
  291.9 6.4 %fusion.13 = bf16[32,2,16,2,64]{4,2,3,1,0:T(8,128)(2,1)S(1)} fusion(bf16[32,512,2,16,2,1]{1,3,4,5,2,0:T(8,128)(2,1)S(1)} %copy.1621, bf16[1,32,1,512,2,64]{3,5,2,4,1,0:T(8,128)(2,1)} %get-tuple-element.8, bf16[1,32,1,512,2,64]{3,5,2,4,1,0:T(8,128)(2,1)} %get-tuple-element.7), kind=kOutput, calls=%fused_computation.28 | convolution fusion | flops 285343744 | bytes 10747904 | tf_op jit(solution)/shard_map/cspfoe,ecosrb->ecpfrb/dot_general | solution.py:90
  (108 shorter events, 71.8 us)
Async XLA Ops:
  5.6 36.0 %collective-permute-start = (bf16[4,2,2,11,32,128]{5,4,2,3,1,0:T(8,128)(2,1)S(1)}, bf16[4,2,2,11,32,128]{5,4,2,3,1,0:T(8,128)(2,1)}, u32[]{:S(2)}, u32[]{:S(2)}) collective-permute-start(bf16[4,2,2,11,32,128]{5,4,2,3,1,0:T(8,128)(2,1)S(1)} %copy.1636), channel_id=1, source_target_pairs={{0,1},{2,3},{4,5},{6,7},{8,9},{10,11},{12,13},{14,15},{16,17},{18,... | collective-permute-start | bytes 4325384 | tf_op jit(solution)/shard_map/ppermute | solution.py:13
  48.8 1.1 copy-start.2
  61.6 94.2 %copy-start = (bf16[32,4,2,16,256]{0,3,4,2,1:T(8,128)(2,1)S(1)}, bf16[32,4,2,16,256]{0,3,4,2,1:T(8,128)(2,1)}, u32[]{:S(2)}) copy-start(bf16[32,4,2,16,256]{0,3,4,2,1:T(8,128)(2,1)} %copy.1626) | copy-start | bytes 6291460
  185.9 38.0 %copy-start.3 = (s32[512]{0:T(512)S(1)}, s32[512]{0:T(512)}, u32[]{:S(2)}) copy-start(s32[512]{0:T(512)} %param.7) | copy-start | bytes 6148
  185.9 38.0 %copy-start.1 = (s32[64,512]{1,0:T(8,128)S(1)}, s32[64,512]{1,0:T(8,128)}, u32[]{:S(2)}) copy-start(s32[64,512]{1,0:T(8,128)} %param.6) | copy-start | bytes 393220
  208.8 66.9 %all-to-all-start = ((bf16[128,2,4096]{2,1,0:T(2,128)(2,1)}), bf16[128,2,4096]{2,1,0:T(2,128)(2,1)S(1)}, u32[]{:S(2)}, u32[]{:S(2)}) async-start(bf16[128,2,4096]{2,1,0:T(2,128)(2,1)} %reshape.376), calls=%async_computation | async-start | bytes 4194304 | tf_op jit(solution)/shard_map/all_to_all | solution.py:87
